TPU v7x, 32 devices: a whole 2x2x4 slice. The times are simulated.
32 devices in a mesh: groups: 2 (over x), loop: 16 (over z, y, core).
Axes of the slice: x: 2, y: 2, z: 4, core: 2. Of those that a mesh axis runs over, the one named last changes fastest.
Arguments:
- real: bfloat16 [32768, 256], P(('groups', 'loop')), parts along dimension 0, may hold values from -0.16 to 0.16
- generated: bfloat16 [32768, 256], P(('groups', 'loop')), parts along dimension 0, may hold values from -0.16 to 0.16
- real_potential: float32 [32768], P(('groups', 'loop')), parts along dimension 0, may hold values from 0.65 to 0.75
- generated_potential: float32 [32768], P(('groups', 'loop')), parts along dimension 0, may hold values from 0.65 to 0.75
Outputs:
- grad_real: bfloat16 [32768, 256], P(('groups', 'loop')), parts along dimension 0
- grad_generated: bfloat16 [32768, 256], P(('groups', 'loop')), parts along dimension 0
There are 2 independent parts, one for each index of `groups`. A program takes and returns all parts, laid end to end along the dimension named above; each array names one. Nothing has to cross between parts.
All inputs are finite; a program needn't handle non-finite values.
Results may differ from a plain program's by a relative error of at most 0.0034.
Values may be sent and summed in bfloat16 or wider, within the bound.
A program may use at most 64 MiB of HBM per device.

v0:
```python
import jax
import jax.numpy as jnp
from jax import lax
from jax.sharding import PartitionSpec as P

WINDOW = 4


epsilon = 0.05


def shifted(block, axis, distance):
    devices = range(lax.axis_size(axis))
    route = [((i - distance) % len(devices), i) for i in devices]
    return lax.ppermute(block, axis, route)


def kernel_tile(left, left_pot, right, right_pot):
    inner = lax.dot_general(
        left, right, (((1,), (1,)), ((), ())), preferred_element_type=jnp.float32
    )
    return jnp.exp((left_pot[:, None] + right_pot[None, :] - 1.0 + inner) / epsilon).astype(
        jnp.bfloat16
    )


def times_points(kernel, points):
    return jnp.dot(kernel, points, preferred_element_type=jnp.float32)


def columns_times(kernel, points):
    return lax.dot_general(
        kernel, points, (((0,), (0,)), ((), ())), preferred_element_type=jnp.float32
    )


def advance_points(points):
    return shifted(points, "loop", 1)


def body(real, generated, real_potential, generated_potential):
    count = lax.axis_size("loop")
    total_rows = real.shape[0] * count
    zeros = jnp.zeros(real.shape, jnp.float32)
    points, potential = (generated, generated_potential)
    gen_sum, real_sum = (zeros, zeros)
    for step in range(WINDOW):
        kernel = kernel_tile(real, real_potential, points, potential)
        real_sum = real_sum + times_points(kernel, points)
        gen_sum = gen_sum + columns_times(kernel, real)
        if step + 1 < WINDOW:
            points = advance_points(points)
            potential, gen_sum = shifted((potential, gen_sum), "loop", 1)
    gen_sum = shifted(gen_sum.astype(jnp.bfloat16), "loop", 1 - WINDOW).astype(gen_sum.dtype)
    grad_real = (-real_sum / total_rows).astype(jnp.bfloat16)
    grad_generated = (-gen_sum / total_rows).astype(jnp.bfloat16)
    return (grad_real, grad_generated)


def solution(mesh):
    in_specs = (
        P(("groups", "loop"), None),
        P(("groups", "loop"), None),
        P(("groups", "loop")),
        P(("groups", "loop")),
    )
    out_specs = (P(("groups", "loop"), None), P(("groups", "loop"), None))
    return jax.shard_map(body, mesh=mesh, in_specs=in_specs, out_specs=out_specs, check_vma=False)
```

profile of v0, /device:TPU:0, one launch (start us, length us, event | category | flops | bytes accessed | tf_op | source)
XLA Modules:
  0.0 90.1 jit_solution(14194278041297758909)
XLA Ops:
  0.6 0.0 copy-start
  0.6 0.5 collective-permute-start.1
  1.1 0.5 copy-done
  1.7 2.1 %exponential_convert_fusion.3 = bf16[1024,1024]{1,0:T(8,128)(2,1)S(1)} fusion(bf16[1024,256]{1,0:T(8,128)(2,1)S(1)} %copy-done, bf16[1024,256]{1,0:T(8,128)(2,1)} %param.5, f32[1024]{0:T(1024)} %param.7, f32[1024]{0:T(1024)} %param.6), kind=kOutput, calls=%fused_computation.3 | convolution fusion | flops 542113792 | bytes 3153920 | tf_op jit(solution)/shard_map/dot_general | solution.py:19
  3.8 0.0 copy-start.2
  3.8 0.0 copy-start.3
  3.8 0.7 fusion.7
  4.6 2.2 %collective-permute-start.6 = (f32[1024,256]{1,0:T(8,128)S(1)}, f32[1024,256]{1,0:T(8,128)S(1)}, u32[]{:S(2)}, u32[]{:S(2)}) collective-permute-start(f32[1024,256]{1,0:T(8,128)S(1)} %fusion.7), channel_id=1, source_target_pairs={{15,0},{0,1},{1,2},{2,3},{3,4},{4,5},{5,6},{6,7},{7,8},{8,9},{9,10... | collective-permute-start | bytes 3145736 | tf_op jit(solution)/shard_map/ppermute | solution.py:15
  6.8 6.5 %collective-permute-done.1 = bf16[1024,256]{1,0:T(8,128)(2,1)S(1)} collective-permute-done((bf16[1024,256]{1,0:T(8,128)(2,1)}, bf16[1024,256]{1,0:T(8,128)(2,1)S(1)}, u32[]{:S(2)}, u32[]{:S(2)}) %collective-permute-start.1) | collective-permute-done | bytes 524320 | tf_op jit(solution)/shard_map/ppermute | solution.py:15
  13.2 0.0 collective-permute-start.3
  13.2 0.0 copy-done.2
  13.2 0.0 collective-permute-start
  13.2 0.7 fusion.5
  14.0 16.1 %collective-permute-done.3 = bf16[1024,256]{1,0:T(8,128)(2,1)S(1)} collective-permute-done((bf16[1024,256]{1,0:T(8,128)(2,1)S(1)}, bf16[1024,256]{1,0:T(8,128)(2,1)S(1)}, u32[]{:S(2)}, u32[]{:S(2)}) %collective-permute-start.3) | collective-permute-done | bytes 524320 | tf_op jit(solution)/shard_map/ppermute | solution.py:15
  30.1 0.0 collective-permute-start.5
  30.1 0.0 collective-permute-done
  30.1 0.0 collective-permute-done.6
  30.1 0.0 copy-done.3
  30.1 1.3 %convolution_add_fusion = f32[1024,256]{1,0:T(8,128)S(1)} fusion(f32[1024,256]{1,0:T(8,128)S(1)} %collective-permute-done.6, bf16[1024,256]{1,0:T(8,128)(2,1)S(1)} %copy-done, f32[1024,1024]{1,0:T(8,128)S(1)} %fusion.5, f32[1024]{0:T(1024)S(1)} %collective-permute-done, f32[1024]{0:T(1024)S(1)} %copy-done.3), kind=kOutput, calls=%fused_computation.4 | convolution fusion | flops 542375936 | bytes 6823936 | tf_op jit(solution)/shard_map/dot_general | solution.py:32
  31.4 0.1 collective-permute-start.7
  31.5 0.1 collective-permute-start.2
  31.6 21.1 %collective-permute-done.2 = f32[1024]{0:T(1024)S(1)} collective-permute-done((f32[1024]{0:T(1024)S(1)}, f32[1024]{0:T(1024)S(1)}, u32[]{:S(2)}, u32[]{:S(2)}) %collective-permute-start.2) | collective-permute-done | bytes 4128 | tf_op jit(solution)/shard_map/ppermute | solution.py:15
  52.7 0.0 collective-permute-start.4
  52.7 0.7 fusion.6
  53.4 5.0 %collective-permute-done.4 = f32[1024]{0:T(1024)S(1)} collective-permute-done((f32[1024]{0:T(1024)S(1)}, f32[1024]{0:T(1024)S(1)}, u32[]{:S(2)}, u32[]{:S(2)}) %collective-permute-start.4) | collective-permute-done | bytes 4128 | tf_op jit(solution)/shard_map/ppermute | solution.py:15
  58.4 0.0 collective-permute-done.5
  58.4 2.2 %exponential_convert_fusion = (bf16[1024,1024]{1,0:T(8,128)(2,1)S(1)}, bf16[1024,1024]{1,0:T(8,128)(2,1)S(1)}) fusion(f32[1024]{0:T(1024)S(1)} %collective-permute-done.4, f32[1024]{0:T(1024)S(1)} %copy-done.3, f32[1024,1024]{1,0:T(8,128)S(1)} %fusion.6, f32[1024]{0:T(1024)S(1)} %collective-permute-done.2, bf16[1024,256]{1,0:T(8,128)(2,1)S(1)} %copy-done, ...), kind=kOutput, calls=%fused_computation | convolution fusion | flops 547356672 | bytes 9449472 | tf_op jit(solution)/shard_map/dot_general | solution.py:19
  60.6 0.0 copy-start.1
  60.6 0.0 collective-permute-done.7
  60.6 0.7 fusion.3
  61.4 0.1 collective-permute-start.8
  61.4 0.2 copy-done.1
  61.7 0.7 fusion.4
  62.4 1.2 %convolution_add_fusion.3 = f32[1024,256]{1,0:T(8,128)S(1)} fusion(f32[1024,256]{1,0:T(8,128)S(1)} %fusion.4, bf16[1024,256]{1,0:T(8,128)(2,1)S(1)} %collective-permute-done.1, f32[1024,1024]{1,0:T(8,128)S(1)} %fusion.5, f32[1024]{0:T(1024)S(1)} %collective-permute-done, f32[1024]{0:T(1024)S(1)} %copy-done.3), kind=kOutput, calls=%fused_computation.9 | convolution fusion | flops 542375936 | bytes 6823936 | tf_op jit(solution)/shard_map/dot_general | solution.py:28
  63.5 16.3 %collective-permute-done.8 = f32[1024,256]{1,0:T(8,128)S(1)} collective-permute-done((f32[1024,256]{1,0:T(8,128)S(1)}, f32[1024,256]{1,0:T(8,128)S(1)}, u32[]{:S(2)}, u32[]{:S(2)}) %collective-permute-start.8) | collective-permute-done | bytes 1048608 | tf_op jit(solution)/shard_map/ppermute | solution.py:15
  79.8 0.8 add_convert_fusion
  80.6 0.1 collective-permute-start.9
  80.7 0.7 convolution_add_fusion.2
  81.4 1.5 %fusion.2 = bf16[1024,256]{1,0:T(8,128)(2,1)} fusion(f32[1024,256]{1,0:T(8,128)S(1)} %convolution_add_fusion.2, bf16[1024,1024]{1,0:T(8,128)(2,1)S(1)} %get-tuple-element.2, bf16[1024,256]{1,0:T(8,128)(2,1)S(1)} %collective-permute-done.5), kind=kOutput, calls=%fused_computation.10 | convolution fusion | flops 537919488 | bytes 4194304 | tf_op jit(solution)/shard_map/dot_general | solution.py:28
  82.9 6.3 %collective-permute-done.9 = bf16[1024,256]{1,0:T(8,128)(2,1)S(1)} collective-permute-done((bf16[1024,256]{1,0:T(8,128)(2,1)S(1)}, bf16[1024,256]{1,0:T(8,128)(2,1)S(1)}, u32[]{:S(2)}, u32[]{:S(2)}) %collective-permute-start.9) | collective-permute-done | bytes 524320 | tf_op jit(solution)/shard_map/ppermute | solution.py:15
  89.2 0.9 multiply_convert_fusion
Async XLA Ops:
  0.6 1.0 %copy-start = (bf16[1024,256]{1,0:T(8,128)(2,1)S(1)}, bf16[1024,256]{1,0:T(8,128)(2,1)}, u32[]{:S(2)}) copy-start(bf16[1024,256]{1,0:T(8,128)(2,1)} %param.4) | copy-start | bytes 1572868
  0.6 12.6 %collective-permute-start.1 = (bf16[1024,256]{1,0:T(8,128)(2,1)}, bf16[1024,256]{1,0:T(8,128)(2,1)S(1)}, u32[]{:S(2)}, u32[]{:S(2)}) collective-permute-start(bf16[1024,256]{1,0:T(8,128)(2,1)} %param.5), channel_id=1, source_target_pairs={{15,0},{0,1},{1,2},{2,3},{3,4},{4,5},{5,6},{6,7},{7,8},{8,9},{9,10... | collective-permute-start | bytes 1572872 | tf_op jit(solution)/shard_map/ppermute | solution.py:15
  3.8 9.4 %copy-start.2 = (f32[1024]{0:T(1024)S(1)}, f32[1024]{0:T(1024)}, u32[]{:S(2)}) copy-start(f32[1024]{0:T(1024)} %param.7) | copy-start | bytes 12292
  3.8 26.3 %copy-start.3 = (f32[1024]{0:T(1024)S(1)}, f32[1024]{0:T(1024)}, u32[]{:S(2)}) copy-start(f32[1024]{0:T(1024)} %param.6) | copy-start | bytes 12292
  4.6 25.5 %collective-permute-start.6 = (f32[1024,256]{1,0:T(8,128)S(1)}, f32[1024,256]{1,0:T(8,128)S(1)}, u32[]{:S(2)}, u32[]{:S(2)}) collective-permute-start(f32[1024,256]{1,0:T(8,128)S(1)} %fusion.7), channel_id=1, source_target_pairs={{15,0},{0,1},{1,2},{2,3},{3,4},{4,5},{5,6},{6,7},{7,8},{8,9},{9,10... | collective-permute-start | bytes 3145736 | tf_op jit(solution)/shard_map/ppermute | solution.py:15
  13.2 16.9 %collective-permute-start.3 = (bf16[1024,256]{1,0:T(8,128)(2,1)S(1)}, bf16[1024,256]{1,0:T(8,128)(2,1)S(1)}, u32[]{:S(2)}, u32[]{:S(2)}) collective-permute-start(bf16[1024,256]{1,0:T(8,128)(2,1)S(1)} %collective-permute-done.1), channel_id=1, source_target_pairs={{15,0},{0,1},{1,2},{2,3},{3,4},{4,5},{5,6},{6,7},{7,8},{8,9},{9,10... | collective-permute-start | bytes 1572872 | tf_op jit(solution)/shard_map/ppermute | solution.py:15
  13.2 16.9 %collective-permute-start = (f32[1024]{0:T(1024)S(1)}, f32[1024]{0:T(1024)S(1)}, u32[]{:S(2)}, u32[]{:S(2)}) collective-permute-start(f32[1024]{0:T(1024)S(1)} %copy-done.2), channel_id=1, source_target_pairs={{15,0},{0,1},{1,2},{2,3},{3,4},{4,5},{5,6},{6,7},{7,8},{8,9},{9,10... | collective-permute-start | bytes 12296 | tf_op jit(solution)/shard_map/ppermute | solution.py:15
  30.1 28.3 %collective-permute-start.5 = (bf16[1024,256]{1,0:T(8,128)(2,1)S(1)}, bf16[1024,256]{1,0:T(8,128)(2,1)S(1)}, u32[]{:S(2)}, u32[]{:S(2)}) collective-permute-start(bf16[1024,256]{1,0:T(8,128)(2,1)S(1)} %collective-permute-done.3), channel_id=1, source_target_pairs={{15,0},{0,1},{1,2},{2,3},{3,4},{4,5},{5,6},{6,7},{7,8},{8,9},{9,10... | collective-permute-start | bytes 1572872 | tf_op jit(solution)/shard_map/ppermute | solution.py:15
  31.4 29.2 %collective-permute-start.7 = (f32[1024,256]{1,0:T(8,128)S(1)}, f32[1024,256]{1,0:T(8,128)S(1)}, u32[]{:S(2)}, u32[]{:S(2)}) collective-permute-start(f32[1024,256]{1,0:T(8,128)S(1)} %convolution_add_fusion), channel_id=1, source_target_pairs={{15,0},{0,1},{1,2},{2,3},{3,4},{4,5},{5,6},{6,7},{7,8},{8,9},{9,10... | collective-permute-start | bytes 3145736 | tf_op jit(solution)/shard_map/ppermute | solution.py:15
  31.5 21.1 %collective-permute-start.2 = (f32[1024]{0:T(1024)S(1)}, f32[1024]{0:T(1024)S(1)}, u32[]{:S(2)}, u32[]{:S(2)}) collective-permute-start(f32[1024]{0:T(1024)S(1)} %collective-permute-done), channel_id=1, source_target_pairs={{15,0},{0,1},{1,2},{2,3},{3,4},{4,5},{5,6},{6,7},{7,8},{8,9},{9,10... | collective-permute-start | bytes 12296 | tf_op jit(solution)/shard_map/ppermute | solution.py:15
  52.7 5.7 %collective-permute-start.4 = (f32[1024]{0:T(1024)S(1)}, f32[1024]{0:T(1024)S(1)}, u32[]{:S(2)}, u32[]{:S(2)}) collective-permute-start(f32[1024]{0:T(1024)S(1)} %collective-permute-done.2), channel_id=1, source_target_pairs={{15,0},{0,1},{1,2},{2,3},{3,4},{4,5},{5,6},{6,7},{7,8},{8,9},{9,10... | collective-permute-start | bytes 12296 | tf_op jit(solution)/shard_map/ppermute | solution.py:15
  60.6 1.0 %copy-start.1 = (bf16[1024,256]{1,0:T(8,128)(2,1)S(1)}, bf16[1024,256]{1,0:T(8,128)(2,1)}, u32[]{:S(2)}) copy-start(bf16[1024,256]{1,0:T(8,128)(2,1)} %param.5) | copy-start | bytes 1572868
  61.4 18.4 %collective-permute-start.8 = (f32[1024,256]{1,0:T(8,128)S(1)}, f32[1024,256]{1,0:T(8,128)S(1)}, u32[]{:S(2)}, u32[]{:S(2)}) collective-permute-start(f32[1024,256]{1,0:T(8,128)S(1)} %fusion.3), channel_id=1, source_target_pairs={{15,0},{0,1},{1,2},{2,3},{3,4},{4,5},{5,6},{6,7},{7,8},{8,9},{9,10... | collective-permute-start | bytes 3145736 | tf_op jit(solution)/shard_map/ppermute | solution.py:15
  80.6 8.7 %collective-permute-start.9 = (bf16[1024,256]{1,0:T(8,128)(2,1)S(1)}, bf16[1024,256]{1,0:T(8,128)(2,1)S(1)}, u32[]{:S(2)}, u32[]{:S(2)}) collective-permute-start(bf16[1024,256]{1,0:T(8,128)(2,1)S(1)} %add_convert_fusion), channel_id=1, source_target_pairs={{3,0},{4,1},{5,2},{6,3},{7,4},{8,5},{9,6},{10,7},{11,8},{12,9},{13... | collective-permute-start | bytes 1572872 | tf_op jit(solution)/shard_map/ppermute | solution.py:15
where the time goes:
time: 90.4 us; the launch traced here: 90.1 us
  waiting for transfers between devices  71.3 us (79%)
  matrix products  13.5 us (15%)
  starting transfers between devices  2.92 us (3%)
    ppermute x10, waiting for transfers between devices, shifted(): return lax.ppermute(block, axis, route)  71.3 us
    dot_general x4, matrix products, kernel_tile(): lax.dot_general(left, right, (((1,), (1,)), ((), ())), preferred_element_...  5.82 us
    dot_general x4, matrix products, times_points(): return jnp.dot(kernel, points, preferred_element_type=jnp.float32)  4.11 us
    dot_general x4, matrix products, columns_times(): lax.dot_general(kernel, points, (((0,), (0,)), ((), ())), preferred_eleme...  3.58 us
    ppermute x10, starting transfers between devices, shifted(): return lax.ppermute(block, axis, route)  2.92 us
  transfers between devices with their start and end apart: 10, of which 6 were waited for; matrix products, arithmetic and copies ran while one was open for 13% of the time, Pallas kernels for 0%

commit v1 on v0

v1 whole, which is shorter than its diff:
```python
import functools

import jax
import jax.numpy as jnp
from jax import lax
from jax.experimental import pallas as pl
from jax.experimental.pallas import tpu as pltpu
from jax.sharding import PartitionSpec as P

WINDOW = 4
epsilon = 0.05
CHUNK = 256
TILE = 256


def kernel(
    n,
    real_ref, gen_ref, real_pot_ref, gen_pot_ref, out_real_ref, out_gen_ref,
    held, pots, columns, acc,
    load_sem, send_sem, recv_sem, pot_send_sem, pot_recv_sem,
):
    rows, width = real_ref.shape
    chunks = rows // CHUNK
    me = lax.axis_index("loop")
    odd = lax.rem(me, 2)
    mate = me + 1 - 2 * odd
    first, second = 1 - odd, odd

    loads = [
        pltpu.make_async_copy(gen_ref, held.at[0, 0], load_sem.at[0]),
        pltpu.make_async_copy(real_ref, held.at[1, 0], load_sem.at[1]),
    ]
    for load in loads:
        load.start()

    def other(distance):
        return lax.rem(me + distance + n, n)

    barrier = pltpu.get_barrier_semaphore()
    for distance in (1, 2, 3, -1, -2, -3):
        pl.semaphore_signal(
            barrier, inc=1, device_id={"loop": other(distance)},
            device_id_type=pl.DeviceIdType.MESH,
        )
    pots[0] = (gen_pot_ref[...] - 0.5) * (1.0 / epsilon)
    pots[4] = (real_pot_ref[...] - 0.5) * (1.0 / epsilon)
    for side in range(2):
        own = pots[4 * (1 - side)]
        columns[side] = jnp.transpose(jnp.broadcast_to(own, (128, rows)))
    acc[...] = jnp.zeros_like(acc)
    pl.semaphore_wait(barrier, 6)

    def block_copy(side, source, c, target, slot, kind):
        part = pl.ds(pl.multiple_of(c * CHUNK, CHUNK), CHUNK)
        return pltpu.make_async_remote_copy(
            src_ref=held.at[side, source, part],
            dst_ref=held.at[side, slot, part],
            send_sem=send_sem.at[side, kind, c],
            recv_sem=recv_sem.at[side, slot, c],
            device_id={"loop": target},
            device_id_type=pl.DeviceIdType.MESH,
        )

    def pot_copy(side, k):
        return pltpu.make_async_remote_copy(
            src_ref=pots.at[4 * side],
            dst_ref=pots.at[4 * side + k],
            send_sem=pot_send_sem.at[side, k - 1],
            recv_sem=pot_recv_sem.at[side, k - 1],
            device_id={"loop": other(k if side == 0 else -k)},
            device_id_type=pl.DeviceIdType.MESH,
        )

    def to_mate(c):
        return block_copy(second, 0, c, mate, 1, 1)

    def by_two(side, c):
        return block_copy(side, 0, c, other(2 - 4 * side), 2, 0)

    def by_three(c):
        return block_copy(first, 0, c, other(3 - 6 * first), 3, 1)

    def onward(which, c):
        if which == 0:
            return block_copy(first, 2, c, mate, 1, 2)
        return block_copy(second, 2, c, mate, 3, 2)

    for load in loads:
        load.wait()
    for side in range(2):
        for k in range(1, WINDOW):
            pot_copy(side, k).start()

    @pl.loop(0, chunks)
    def _(c):
        to_mate(c).start()
        by_two(0, c).start()
        by_two(1, c).start()
        by_three(c).start()

    def piece(side, slot, c):
        part = pl.ds(pl.multiple_of(c * CHUNK, CHUNK), CHUNK)
        points = held[side, slot, part]
        row = pots[4 * side + slot, :, part]
        for start in range(0, rows, TILE):
            tile = pl.ds(start, TILE)
            inner = lax.dot_general(
                held[1 - side, 0, tile], points, (((1,), (1,)), ((), ())),
                preferred_element_type=jnp.float32,
            )
            column = columns[side, tile]
            column = jnp.concatenate([column] * (CHUNK // 128), axis=1)
            weights = jnp.exp(inner * (1.0 / epsilon) + (column + row))
            acc[side, tile] += jnp.dot(
                weights.astype(jnp.bfloat16), points, preferred_element_type=jnp.float32
            )

    @pl.loop(0, chunks)
    def _(c):
        piece(0, 0, c)
        piece(1, 0, c)

    for side in range(2):
        for k in range(1, WINDOW):
            pot_copy(side, k).wait_recv()

    def arrived(side, slot, c):
        block_copy(side, 0, c, mate, slot, 0).wait_recv()

    @pl.loop(0, chunks)
    def _(c):
        arrived(first, 1, c)
        piece(first, 1, c)

    @pl.loop(0, chunks)
    def _(c):
        arrived(first, 2, c)
        onward(0, c).start()
        arrived(second, 2, c)
        onward(1, c).start()
        piece(first, 2, c)
        piece(second, 2, c)
        arrived(second, 3, c)
        piece(second, 3, c)
        arrived(second, 1, c)
        piece(second, 1, c)
        arrived(first, 3, c)
        piece(first, 3, c)

    scale = -1.0 / (rows * n)
    out_real_ref[...] = (acc[0] * scale).astype(out_real_ref.dtype)
    out_gen_ref[...] = (acc[1] * scale).astype(out_gen_ref.dtype)

    for side in range(2):
        for k in range(1, WINDOW):
            pot_copy(side, k).wait_send()

    @pl.loop(0, chunks)
    def _(c):
        to_mate(c).wait_send()
        by_two(0, c).wait_send()
        by_two(1, c).wait_send()
        by_three(c).wait_send()
        onward(0, c).wait_send()
        onward(1, c).wait_send()


def body(real, generated, real_potential, generated_potential):
    rows, width = real.shape
    n = lax.axis_size("loop")
    chunks = rows // CHUNK
    any_space = pl.BlockSpec(memory_space=pl.ANY)
    vmem = pl.BlockSpec(memory_space=pltpu.VMEM)
    out = jax.ShapeDtypeStruct((rows, width), jnp.bfloat16)
    pairs = 2 * WINDOW * rows * rows
    return pl.pallas_call(
        functools.partial(kernel, n),
        out_shape=(out, out),
        in_specs=[any_space, any_space, vmem, vmem],
        out_specs=(vmem, vmem),
        scratch_shapes=[
            pltpu.VMEM((2, WINDOW, rows, width), jnp.bfloat16),
            pltpu.VMEM((2 * WINDOW, 1, rows), jnp.float32),
            pltpu.VMEM((2, rows, 128), jnp.float32),
            pltpu.VMEM((2, rows, width), jnp.float32),
            pltpu.SemaphoreType.DMA((2,)),
            pltpu.SemaphoreType.DMA((2, 3, chunks)),
            pltpu.SemaphoreType.DMA((2, WINDOW, chunks)),
            pltpu.SemaphoreType.DMA((2, WINDOW - 1)),
            pltpu.SemaphoreType.DMA((2, WINDOW - 1)),
        ],
        compiler_params=pltpu.CompilerParams(
            collective_id=0, has_side_effects=True, vmem_limit_bytes=40 * 1024 * 1024
        ),
        cost_estimate=pl.CostEstimate(
            flops=4 * pairs * width, bytes_accessed=8 * rows * width, transcendentals=pairs
        ),
    )(real, generated, real_potential.reshape(1, rows), generated_potential.reshape(1, rows))


def solution(mesh):
    in_specs = (
        P(("groups", "loop"), None),
        P(("groups", "loop"), None),
        P(("groups", "loop")),
        P(("groups", "loop")),
    )
    out_specs = (P(("groups", "loop"), None), P(("groups", "loop"), None))
    return jax.shard_map(body, mesh=mesh, in_specs=in_specs, out_specs=out_specs, check_vma=False)
```

time: 90.4 us -> 38.4 us (0.42)
  waiting for transfers between devices: 71.3 us -> 0 us
  Pallas kernels: 0 us -> 32.4 us
  matrix products: 13.5 us -> 0 us
  local copies, waits for them, and re-layouts: 0.76 us -> 5.04 us
  starting transfers between devices: 2.92 us -> 0 us
    ppermute x10 -> x0, waiting for transfers between devices: 71.3 us -> none  [shifted(): return lax.ppermute(block, axis, route)]
    pallas_call x0 -> x1, Pallas kernels: none -> 32.4 us  [body(): pl.pallas_call(functools.partial(kernel, n), out_shape=(out, out), in_spe...]
    dot_general x12 -> x0, matrix products: 13.5 us -> none  [the longest x4 5.82 us: kernel_tile(): lax.dot_general(left, right, (((1,), (1,)), ((), ())), preferred_element_...]
    unnamed x8 -> x10, local copies, waits for them, and re-layouts: 0.76 us -> 5.04 us
    ppermute x10 -> x0, starting transfers between devices: 2.92 us -> none  [shifted(): return lax.ppermute(block, axis, route)]
  transfers between devices with their start and end apart: 10 -> 0, of which waited for: 6 -> 0; matrix products, arithmetic and copies ran while one was open for 13% -> 0% of each run, Pallas kernels for 0% -> 0%
where the time goes in v1:
time: 38.4 us; the launch traced here: 38.1 us
  Pallas kernels  32.4 us (84%)
  local copies, waits for them, and re-layouts  5.04 us (13%)
  between operations  0.65 us (2%)
    pallas_call x1, Pallas kernels, body(): pl.pallas_call(functools.partial(kernel, n), out_shape=(out, out), in_spe...  32.4 us
    unnamed x10, local copies, waits for them, and re-layouts  5.04 us

profile of v1, /device:TPU:0, one launch (start us, length us, event | category | flops | bytes accessed | tf_op | source)
XLA Modules:
  0.0 38.1 jit_solution(15303378945615015441)
XLA Ops:
  0.6 0.0 copy-start
  0.6 1.0 %copy-done = bf16[1024,256]{1,0:T(8,128)(2,1)S(1)} copy-done((bf16[1024,256]{1,0:T(8,128)(2,1)S(1)}, bf16[1024,256]{1,0:T(8,128)(2,1)}, u32[]{:S(2)}) %copy-start) | copy-done | bytes 524312
  1.7 0.0 copy-start.1
  1.7 1.0 %copy-done.1 = bf16[1024,256]{1,0:T(8,128)(2,1)S(1)} copy-done((bf16[1024,256]{1,0:T(8,128)(2,1)S(1)}, bf16[1024,256]{1,0:T(8,128)(2,1)}, u32[]{:S(2)}) %copy-start.1) | copy-done | bytes 524312
  2.7 0.0 copy-start.2
  2.7 0.7 %copy-done.2 = f32[1024]{0:T(1024)S(1)} copy-done((f32[1024]{0:T(1024)S(1)}, f32[1024]{0:T(1024)}, u32[]{:S(2)}) %copy-start.2) | copy-done | bytes 4120
  3.4 0.0 copy-start.3
  3.4 0.7 %copy-done.3 = f32[1024]{0:T(1024)S(1)} copy-done((f32[1024]{0:T(1024)S(1)}, f32[1024]{0:T(1024)}, u32[]{:S(2)}) %copy-start.3) | copy-done | bytes 4120
  4.1 32.4 %shard_map.59 = (bf16[1024,256]{1,0:T(8,128)(2,1)S(1)}, bf16[1024,256]{1,0:T(8,128)(2,1)S(1)}) custom-call(bf16[1024,256]{1,0:T(8,128)(2,1)S(1)} %copy-done, bf16[1024,256]{1,0:T(8,128)(2,1)S(1)} %copy-done.1, f32[1,1024]{1,0:T(1,128)S(1)} %bitcast.2, f32[1,1024]{1,0:T(1,128)S(1)} %bitcast.3), custom_call_target="tpu_custom_call" | custom-call | flops 8589934592 | bytes 2097152 | tf_op jit(solution)/shard_map/pallas_call | solution.py:176
  36.5 0.8 %copy.8 = bf16[1024,256]{1,0:T(8,128)(2,1)} copy(bf16[1024,256]{1,0:T(8,128)(2,1)S(1)} %get-tuple-element.4) | data formatting | bytes 1048576
  37.3 0.8 %copy.9 = bf16[1024,256]{1,0:T(8,128)(2,1)} copy(bf16[1024,256]{1,0:T(8,128)(2,1)S(1)} %get-tuple-element.5) | data formatting | bytes 1048576
Async XLA Ops:
  0.6 1.0 %copy-start = (bf16[1024,256]{1,0:T(8,128)(2,1)S(1)}, bf16[1024,256]{1,0:T(8,128)(2,1)}, u32[]{:S(2)}) copy-start(bf16[1024,256]{1,0:T(8,128)(2,1)} %real_ref.1) | copy-start | bytes 1572868
  1.7 1.0 %copy-start.1 = (bf16[1024,256]{1,0:T(8,128)(2,1)S(1)}, bf16[1024,256]{1,0:T(8,128)(2,1)}, u32[]{:S(2)}) copy-start(bf16[1024,256]{1,0:T(8,128)(2,1)} %gen_ref.1) | copy-start | bytes 1572868
  2.7 0.7 %copy-start.2 = (f32[1024]{0:T(1024)S(1)}, f32[1024]{0:T(1024)}, u32[]{:S(2)}) copy-start(f32[1024]{0:T(1024)} %param.6) | copy-start | bytes 12292
  3.4 0.7 %copy-start.3 = (f32[1024]{0:T(1024)S(1)}, f32[1024]{0:T(1024)}, u32[]{:S(2)}) copy-start(f32[1024]{0:T(1024)} %param.7) | copy-start | bytes 12292

commit v2 on v1

v2 whole, which is shorter than its diff:
```python
import functools

import jax
import jax.numpy as jnp
from jax import lax
from jax.experimental import pallas as pl
from jax.experimental.pallas import tpu as pltpu
from jax.sharding import PartitionSpec as P

WINDOW = 4
epsilon = 0.05
CHUNK = 256
TILE = 256


def kernel(
    n,
    real_ref, gen_ref, real_pot_ref, gen_pot_ref, out_ref,
    held, raw, pots, columns, acc,
    load_sem, send_sem, recv_sem, pot_send_sem, pot_recv_sem,
):
    rows, width = real_ref.shape
    chunks = rows // CHUNK
    me = lax.axis_index("loop")
    odd = lax.rem(me, 2)
    mate = me + 1 - 2 * odd
    first, second = 1 - odd, odd

    loads = [
        pltpu.make_async_copy(gen_pot_ref, raw.at[0], load_sem.at[0]),
        pltpu.make_async_copy(real_pot_ref, raw.at[1], load_sem.at[1]),
        pltpu.make_async_copy(gen_ref, held.at[0, 0], load_sem.at[2]),
        pltpu.make_async_copy(real_ref, held.at[1, 0], load_sem.at[3]),
    ]
    for load in loads:
        load.start()

    def other(distance):
        return lax.rem(me + distance + n, n)

    barrier = pltpu.get_barrier_semaphore()
    for distance in (1, 2, 3, -1, -2, -3):
        pl.semaphore_signal(
            barrier, inc=1, device_id={"loop": other(distance)},
            device_id_type=pl.DeviceIdType.MESH,
        )
    loads[0].wait()
    loads[1].wait()
    pots[0] = (raw[0] - 0.5) * (1.0 / epsilon)
    pots[4] = (raw[1] - 0.5) * (1.0 / epsilon)
    pl.semaphore_wait(barrier, 6)

    def block_copy(side, c, target, slot, kind, source=None):
        part = pl.ds(pl.multiple_of(c * CHUNK, CHUNK), CHUNK)
        return pltpu.make_async_remote_copy(
            src_ref=held.at[side, 2, part] if source is None else source.at[part],
            dst_ref=held.at[side, slot, part],
            send_sem=send_sem.at[side, kind, c],
            recv_sem=recv_sem.at[side, slot, c],
            device_id={"loop": target},
            device_id_type=pl.DeviceIdType.MESH,
        )

    def pot_copy(side, k):
        return pltpu.make_async_remote_copy(
            src_ref=pots.at[4 * side],
            dst_ref=pots.at[4 * side + k],
            send_sem=pot_send_sem.at[side, k - 1],
            recv_sem=pot_recv_sem.at[side, k - 1],
            device_id={"loop": other(k if side == 0 else -k)},
            device_id_type=pl.DeviceIdType.MESH,
        )

    def by_two(side, c):
        return block_copy(side, c, other(2 - 4 * side), 2, 0, (gen_ref, real_ref)[side])

    def to_mate(side, c):
        return block_copy(side, c, mate, 1, 1, (gen_ref, real_ref)[side])

    def by_three(side, c):
        return block_copy(side, c, other(3 - 6 * side), 3, 1, (gen_ref, real_ref)[side])

    def onward(which, c):
        if which == 0:
            return block_copy(first, c, mate, 1, 2)
        return block_copy(second, c, mate, 3, 2)

    for side in range(2):
        for k in range(1, WINDOW):
            pot_copy(side, k).start()

    @pl.loop(0, chunks)
    def _(c):
        by_two(0, c).start()
        by_two(1, c).start()
        for side in range(2):

            @pl.when(second == side)
            def _():
                by_three(1 - side, c).start()
                to_mate(side, c).start()

    acc[...] = jnp.zeros_like(acc)
    for side in range(2):
        own = pots[4 * (1 - side)]
        columns[side] = jnp.transpose(jnp.broadcast_to(own, (128, rows)))
    loads[2].wait()
    loads[3].wait()

    scale = -1.0 / (rows * n)

    def piece(side, slot, c, last=False):
        part = pl.ds(pl.multiple_of(c * CHUNK, CHUNK), CHUNK)
        points = held[side, slot, part]
        row = pots[4 * side + slot, :, part]
        for start in range(0, rows, TILE):
            tile = pl.ds(start, TILE)
            inner = lax.dot_general(
                held[1 - side, 0, tile], points, (((1,), (1,)), ((), ())),
                preferred_element_type=jnp.float32,
            )
            column = columns[side, tile]
            column = jnp.concatenate([column] * (CHUNK // 128), axis=1)
            weights = jnp.exp(inner * (1.0 / epsilon) + (column + row))
            total = acc[side, tile] + jnp.dot(
                weights.astype(jnp.bfloat16), points, preferred_element_type=jnp.float32
            )
            if last:
                out_ref[side, tile] = (total * scale).astype(out_ref.dtype)
            else:
                acc[side, tile] = total

    @pl.loop(0, chunks)
    def _(c):
        piece(0, 0, c)
        piece(1, 0, c)

    for side in range(2):
        for k in range(1, WINDOW):
            pot_copy(side, k).wait_recv()

    def arrived(side, slot, c):
        block_copy(side, c, mate, slot, 0).wait_recv()

    @pl.loop(0, chunks)
    def _(c):
        arrived(first, 1, c)
        piece(first, 1, c)

    def round_of(c, last):
        arrived(first, 2, c)
        onward(0, c).start()
        arrived(second, 2, c)
        onward(1, c).start()
        arrived(second, 3, c)
        piece(second, 3, c)
        piece(first, 2, c)
        piece(second, 2, c)
        arrived(second, 1, c)
        piece(second, 1, c, last)
        arrived(first, 3, c)
        piece(first, 3, c, last)

    @pl.loop(0, chunks - 1)
    def _(c):
        round_of(c, False)

    round_of(chunks - 1, True)

    for side in range(2):
        for k in range(1, WINDOW):
            pot_copy(side, k).wait_send()

    @pl.loop(0, chunks)
    def _(c):
        by_two(0, c).wait_send()
        by_two(1, c).wait_send()
        for side in range(2):

            @pl.when(second == side)
            def _():
                by_three(1 - side, c).wait_send()
                to_mate(side, c).wait_send()

        onward(0, c).wait_send()
        onward(1, c).wait_send()


def hand_over(both_ref, real_ref, gen_ref, sem):
    copies = [
        pltpu.make_async_copy(both_ref.at[0], real_ref, sem.at[0]),
        pltpu.make_async_copy(both_ref.at[1], gen_ref, sem.at[1]),
    ]
    for copy in copies:
        copy.start()
    for copy in copies:
        copy.wait()


def body(real, generated, real_potential, generated_potential):
    rows, width = real.shape
    n = lax.axis_size("loop")
    chunks = rows // CHUNK
    operands = (
        real, generated, real_potential.reshape(1, rows), generated_potential.reshape(1, rows)
    )
    hbm = pl.BlockSpec(memory_space=pltpu.HBM)
    out = jax.ShapeDtypeStruct((rows, width), jnp.bfloat16)
    pairs = 2 * WINDOW * rows * rows
    both = pl.pallas_call(
        functools.partial(kernel, n),
        out_shape=pltpu.VMEM((2, rows, width), jnp.bfloat16),
        in_specs=[hbm] * 4,
        out_specs=pl.BlockSpec(memory_space=pltpu.VMEM),
        scratch_shapes=[
            pltpu.VMEM((2, WINDOW, rows, width), jnp.bfloat16),
            pltpu.VMEM((2, 1, rows), jnp.float32),
            pltpu.VMEM((2 * WINDOW, 1, rows), jnp.float32),
            pltpu.VMEM((2, rows, 128), jnp.float32),
            pltpu.VMEM((2, rows, width), jnp.float32),
            pltpu.SemaphoreType.DMA((4,)),
            pltpu.SemaphoreType.DMA((2, 3, chunks)),
            pltpu.SemaphoreType.DMA((2, WINDOW, chunks)),
            pltpu.SemaphoreType.DMA((2, WINDOW - 1)),
            pltpu.SemaphoreType.DMA((2, WINDOW - 1)),
        ],
        compiler_params=pltpu.CompilerParams(
            collective_id=0, has_side_effects=True, vmem_limit_bytes=24 * 1024 * 1024
        ),
        cost_estimate=pl.CostEstimate(
            flops=4 * pairs * width, bytes_accessed=8 * rows * width, transcendentals=pairs
        ),
    )(*(pltpu.with_memory_space_constraint(x, pltpu.HBM) for x in operands))
    return pl.pallas_call(
        hand_over,
        out_shape=(out, out),
        in_specs=[pl.BlockSpec(memory_space=pl.ANY)],
        out_specs=(hbm, hbm),
        scratch_shapes=[pltpu.SemaphoreType.DMA((2,))],
        compiler_params=pltpu.CompilerParams(vmem_limit_bytes=24 * 1024 * 1024),
    )(both)


def solution(mesh):
    in_specs = (
        P(("groups", "loop"), None),
        P(("groups", "loop"), None),
        P(("groups", "loop")),
        P(("groups", "loop")),
    )
    out_specs = (P(("groups", "loop"), None), P(("groups", "loop"), None))
    return jax.shard_map(body, mesh=mesh, in_specs=in_specs, out_specs=out_specs, check_vma=False)
```

time: 38.4 us -> 35.2 us (0.917)
  local copies, waits for them, and re-layouts: 5.04 us -> 0 us
  Pallas kernels: 32.4 us -> 34.4 us
    unnamed x10 -> x0, local copies, waits for them, and re-layouts: 5.04 us -> none
    pallas_call x1 -> x2, Pallas kernels: 32.4 us -> 34.4 us  [the longest x1 33.4 us: body(): pl.pallas_call(functools.partial(kernel, n), out_shape=pltpu.VMEM((2, row...]
where the time goes in v2:
time: 35.2 us; the launch traced here: 35 us
  Pallas kernels  34.4 us (98%)
  between operations  0.64 us (2%)
    pallas_call x1, Pallas kernels, body(): pl.pallas_call(functools.partial(kernel, n), out_shape=pltpu.VMEM((2, row...  33.4 us
    pallas_call x1, Pallas kernels, body(): pl.pallas_call(hand_over, out_shape=(out, out), in_specs=[pl.BlockSpec(me...  0.99 us

profile of v2, /device:TPU:0, one launch (start us, length us, event | category | flops | bytes accessed | tf_op | source)
XLA Modules:
  0.0 35.0 jit_solution(12310347105803965838)
XLA Ops:
  0.6 33.4 %shard_map.59.both_ref = bf16[2,1024,256]{2,1,0:T(8,128)(2,1)S(1)} custom-call(bf16[1024,256]{1,0:T(8,128)(2,1)} %real_ref.1, bf16[1024,256]{1,0:T(8,128)(2,1)} %gen_ref.1, f32[1,1024]{1,0:T(1,128)} %bitcast.2, f32[1,1024]{1,0:T(1,128)} %bitcast.3), custom_call_target="tpu_custom_call" | custom-call | flops 8589934592 | bytes 2097152 | tf_op jit(solution)/shard_map/pallas_call | solution.py:210
  34.0 1.0 %shard_map.60 = (bf16[1024,256]{1,0:T(8,128)(2,1)}, bf16[1024,256]{1,0:T(8,128)(2,1)}) custom-call(bf16[2,1024,256]{2,1,0:T(8,128)(2,1)S(1)} %shard_map.59.both_ref), custom_call_target="tpu_custom_call" | custom-call | tf_op jit(solution)/shard_map/pallas_call | solution.py:234

commit v3 on v2

--- a/solution.py
+++ b/solution.py
@@ -10,7 +10,7 @@
 WINDOW = 4
 epsilon = 0.05
 CHUNK = 256
-TILE = 256
+TILE = 512
 
 
 def kernel(
@@ -91,8 +91,6 @@
 
     @pl.loop(0, chunks)
     def _(c):
-        by_two(0, c).start()
-        by_two(1, c).start()
         for side in range(2):
 
             @pl.when(second == side)
@@ -100,6 +98,9 @@
                 by_three(1 - side, c).start()
                 to_mate(side, c).start()
 
+        by_two(0, c).start()
+        by_two(1, c).start()
+
     acc[...] = jnp.zeros_like(acc)
     for side in range(2):
         own = pots[4 * (1 - side)]
@@ -113,12 +114,19 @@
         part = pl.ds(pl.multiple_of(c * CHUNK, CHUNK), CHUNK)
         points = held[side, slot, part]
         row = pots[4 * side + slot, :, part]
-        for start in range(0, rows, TILE):
-            tile = pl.ds(start, TILE)
-            inner = lax.dot_general(
-                held[1 - side, 0, tile], points, (((1,), (1,)), ((), ())),
+
+        def products(start):
+            return lax.dot_general(
+                held[1 - side, 0, pl.ds(start, TILE)], points, (((1,), (1,)), ((), ())),
                 preferred_element_type=jnp.float32,
             )
+
+        ahead = products(0)
+        for start in range(0, rows, TILE):
+            inner = ahead
+            if start + TILE < rows:
+                ahead = products(start + TILE)
+            tile = pl.ds(start, TILE)
             column = columns[side, tile]
             column = jnp.concatenate([column] * (CHUNK // 128), axis=1)
             weights = jnp.exp(inner * (1.0 / epsilon) + (column + row))
@@ -152,8 +160,9 @@
         onward(0, c).start()
         arrived(second, 2, c)
         onward(1, c).start()
-        arrived(second, 3, c)
-        piece(second, 3, c)
+        if not last:
+            arrived(second, 3, c)
+            piece(second, 3, c)
         piece(first, 2, c)
         piece(second, 2, c)
         arrived(second, 1, c)
@@ -165,6 +174,8 @@
     def _(c):
         round_of(c, False)
 
+    arrived(second, 3, chunks - 1)
+    piece(second, 3, chunks - 1)
     round_of(chunks - 1, True)
 
     for side in range(2):

time: 35.2 us -> 34.9 us (level)
  Pallas kernels: 34.4 us -> 34 us
where the time goes in v3:
time: 34.9 us; the launch traced here: 34.7 us
  Pallas kernels  34 us (97%)
  between operations  0.64 us (2%)
    pallas_call x1, Pallas kernels, body(): pl.pallas_call(functools.partial(kernel, n), out_shape=pltpu.VMEM((2, row...  33.1 us
    pallas_call x1, Pallas kernels, body(): pl.pallas_call(hand_over, out_shape=(out, out), in_specs=[pl.BlockSpec(me...  0.99 us

profile of v3, /device:TPU:0, one launch (start us, length us, event | category | flops | bytes accessed | tf_op | source)
XLA Modules:
  0.0 34.7 jit_solution(15861627667513352070)
XLA Ops:
  0.6 33.1 %shard_map.59.both_ref = bf16[2,1024,256]{2,1,0:T(8,128)(2,1)S(1)} custom-call(bf16[1024,256]{1,0:T(8,128)(2,1)} %real_ref.1, bf16[1024,256]{1,0:T(8,128)(2,1)} %gen_ref.1, f32[1,1024]{1,0:T(1,128)} %bitcast.2, f32[1,1024]{1,0:T(1,128)} %bitcast.3), custom_call_target="tpu_custom_call" | custom-call | flops 8589934592 | bytes 2097152 | tf_op jit(solution)/shard_map/pallas_call | solution.py:221
  33.7 1.0 %shard_map.60 = (bf16[1024,256]{1,0:T(8,128)(2,1)}, bf16[1024,256]{1,0:T(8,128)(2,1)}) custom-call(bf16[2,1024,256]{2,1,0:T(8,128)(2,1)S(1)} %shard_map.59.both_ref), custom_call_target="tpu_custom_call" | custom-call | tf_op jit(solution)/shard_map/pallas_call | solution.py:245
